TPU v7x, 512 devices: a whole 4x4x16 slice. The times are simulated.
512 devices in a mesh: section: 8 (over y, core), tensor: 64 (over x, z).
Axes of the slice: x: 4, y: 4, z: 16, core: 2. Of those that a mesh axis runs over, the one named last changes fastest.
Arguments:
- hidden: bfloat16 [2048, 8192], P('section', 'tensor'), may hold values from -6 to 6
- arriving: bfloat16 [256, 8192], P(None, 'tensor'), may hold values from -6 to 6
- ids: int32 [9, 256, 1], replicated, may hold values from 0 to 63; in each aligned block of 256 rows (0 to 255, 256 to 511, ..., all dimensions but the last counted through in order) at most 16 rows name the same one
- adapter_slot: int32 [64], replicated, may hold values from 0 to 63, each once
- base_matrix: bfloat16 [8, 8192, 8192], P('section', None, 'tensor'), may hold values from -0.0625 to 0.0625
- adapter_down: bfloat16 [8, 64, 8192, 64], P('section', 'tensor'), may hold values from -0.0625 to 0.0625
- adapter_up: bfloat16 [8, 64, 64, 8192], P('section', 'tensor'), may hold values from -0.75 to 0.75
Outputs:
- outputs: bfloat16 [2, 2048, 8192], P(None, 'section', 'tensor')
Inputs may be any that keep to these rules, and one draw needn't show every extreme that they name: `ids`: within each microbatch of 256 requests no adapter is named by more than 16 requests, and this bound is reached. A permutation: adapter a sits in store slot adapter_slot[a], on tensor device adapter_slot[a] of its section.
All inputs are finite; a program needn't handle non-finite values.
Results may differ from a plain program's by a relative error of at most 0.012.
Values may be sent and summed in bfloat16 or wider, within the bound.
A program may use at most 64 MiB of HBM per device.

v0:
```python
import jax
import jax.numpy as jnp
from jax import lax
from jax.sharding import PartitionSpec as P

TICKS = 2


def from_behind(value, axis, steps):
    count = lax.axis_size(axis)
    first, last = (max(0, -steps), min(count, count - steps))
    return lax.ppermute(value, axis, [(source, source + steps) for source in range(first, last)])


def local(hidden, arriving, ids, adapter_slot, base_matrix, adapter_down, adapter_up):
    section_index = lax.axis_index("section")
    section_count = lax.axis_size("section")
    tensor_index = lax.axis_index("tensor")
    tensor_count = lax.axis_size("tensor")
    row_count = hidden.shape[0]
    col_count = base_matrix.shape[2]
    hidden_width = base_matrix.shape[1]
    local_slots = adapter_down.shape[1]
    adapter_rank_size = adapter_down.shape[3]
    adapter_ids = local_slots * tensor_count
    weight = base_matrix[0]
    down_flat = jnp.transpose(adapter_down[0], (1, 0, 2)).reshape(
        hidden_width, local_slots * adapter_rank_size
    )
    own_slots = tensor_index * local_slots + jnp.arange(local_slots, dtype=jnp.int32)
    slot_tiles = lax.all_to_all(adapter_up[0], "tensor", split_axis=2, concat_axis=0, tiled=True)
    flattened_tiles = slot_tiles.reshape(adapter_ids * adapter_rank_size, col_count)
    current_state = hidden
    results = []
    for step_index in range(TICKS):
        microbatch_index = jnp.where(
            section_index >= step_index,
            section_index - step_index,
            section_count + step_index - 1 - section_index,
        )
        row_ids = lax.dynamic_index_in_dim(ids, microbatch_index, 0, keepdims=False)[:, 0]
        slot_ids = jnp.take(adapter_slot, row_ids, axis=0)
        shard_part = lax.all_gather(current_state, "tensor", axis=1, tiled=True)
        base_product = jnp.dot(shard_part, weight, preferred_element_type=jnp.float32)
        low_rank = jnp.dot(shard_part, down_flat, preferred_element_type=jnp.float32)
        low_three = low_rank.reshape(row_count, local_slots, adapter_rank_size)
        owned = slot_ids[:, None] == own_slots[None, :]
        full_hot = slot_ids[:, None] == jnp.arange(adapter_ids, dtype=jnp.int32)[None, :]
        mine = jnp.sum(jnp.where(owned[:, :, None], low_three, jnp.zeros((), jnp.float32)), axis=1)
        chosen = lax.psum(mine, "tensor").astype(jnp.bfloat16)
        expanded_rows = jnp.where(
            full_hot[:, :, None], chosen[:, None, :], jnp.zeros((), jnp.bfloat16)
        ).reshape(row_count, adapter_ids * adapter_rank_size)
        adapter_product = jnp.dot(
            expanded_rows, flattened_tiles, preferred_element_type=jnp.float32
        ).astype(jnp.bfloat16)
        layer_out = (
            current_state.astype(jnp.float32) + base_product + adapter_product.astype(jnp.float32)
        ).astype(jnp.bfloat16)
        results.append(layer_out)
        if step_index + 1 < TICKS:
            moved = from_behind(layer_out, "section", 1)
            current_state = jnp.where(section_index == 0, arriving, moved)
    return jnp.stack(results, 0)


def solution(mesh):
    in_specs = (
        P("section", "tensor"),
        P(None, "tensor"),
        P(),
        P(),
        P("section", None, "tensor"),
        P("section", "tensor", None, None),
        P("section", "tensor", None, None),
    )
    out_specs = P(None, "section", "tensor")
    return jax.shard_map(local, mesh=mesh, in_specs=in_specs, out_specs=out_specs, check_vma=False)
```

profile of v0, /device:TPU:8, one launch (start us, length us, event | category | flops | bytes accessed | tf_op | source)
XLA Modules:
  0.0 902.1 jit_solution(13716160890957206217)
XLA Ops:
  6.5 0.0 copy-start
  6.5 0.0 all-gather.3.cloned.1.call-start
  6.5 0.7 all-gather.3.cloned.1.call-update
  7.3 9.2 %copy.14 = bf16[1,64,8192]{1,0,2:T(2,128)(2,1)} copy(bf16[1,64,8192]{2,1,0:T(8,128)(2,1)} %bitcast.53) | data formatting | bytes 2097152 | tf_op jit(solution)/shard_map/squeeze | solution.py:31
  16.5 0.5 broadcast.84
  17.0 46.6 %reduce = bf16[8192,64]{1,0:T(8,128)(2,1)} reduce(bf16[8192,1,64]{2,1,0:T(2,128)(2,1)} %bitcast.45, bf16[]{:T(256)} %broadcast.84), dimensions={1}, to_apply=%bitcast.32.reduce_sub_computation | reduce | bytes 2097154
  63.6 0.0 copy-start.1
  63.6 4.7 reshape.125
  68.3 18.6 %all-to-all-start = ((bf16[64,2,4096]{2,1,0:T(2,128)(2,1)}), bf16[64,2,4096]{2,1,0:T(2,128)(2,1)S(1)}, u32[]{:S(2)}, u32[]{:S(2)}) async-start(bf16[64,2,4096]{2,1,0:T(2,128)(2,1)} %reshape.125), calls=%async_computation | async-start | bytes 2097152 | tf_op jit(solution)/shard_map/all_to_all | solution.py:31
  86.8 0.0 all-gather.5.cloned.1.call-start
  86.9 0.7 constant_dynamic-slice_fusion.1
  87.6 0.0 copy-done.1
  87.6 1.9 gather_fusion
  89.5 56.5 %all-to-all-done = bf16[64,2,4096]{2,1,0:T(2,128)(2,1)S(1)} async-done(((bf16[64,2,4096]{2,1,0:T(2,128)(2,1)}), bf16[64,2,4096]{2,1,0:T(2,128)(2,1)S(1)}, u32[]{:S(2)}, u32[]{:S(2)}) %all-to-all-start) | async-done | bytes 1048608 | tf_op jit(solution)/shard_map/all_to_all | solution.py:31
  146.0 7.0 reshape.126
  153.1 8.2 copy.15
  161.3 0.3 copy.17
  161.5 0.1 bitcast_bitcast_fusion
  161.6 0.7 copy.16
  162.3 22.0 %all-gather.3.cloned.1.call-done = bf16[256,8192]{1,0:T(8,128)(2,1)} async-done(((bf16[256,128]{1,0:T(8,128)(2,1)}), bf16[256,8192]{1,0:T(8,128)(2,1)}) %all-gather.3.cloned.1.call-update) | async-done | bytes 4194320 | tf_op jit(solution)/shard_map/all_gather | solution.py:43
  184.3 3.9 convolution_select_fusion.1
  188.2 278.7 %psum.14 = bf16[256,64]{0,1:T(8,128)(2,1)S(1)} all-reduce(f32[256,64]{0,1:T(8,128)S(1)} %convolution_select_fusion.1), channel_id=1, replica_groups=mesh['section'=8,'tensor'=64] {'tensor'}, use_global_device_ids=true, to_apply=%region_0.2 | all-reduce | flops 16384 | bytes 98304 | tf_op jit(solution)/shard_map/psum | solution.py:50
  466.9 0.0 copy-start.2
  466.9 0.1 broadcast_select_fusion.1
  467.1 0.0 copy-start.5
  467.1 0.8 fusion.10
  467.8 0.0 copy-done
  467.9 1.2 copy-done.2
  469.1 0.0 copy-done.5
  469.1 0.0 copy-start.6
  469.1 1.3 fusion.12
  470.4 1.9 collective-permute-start
  472.3 3.7 collective-permute-done
  476.0 0.0 copy-done.6
  476.0 0.6 broadcast_select_fusion.2
  476.6 0.0 all-gather.5.cloned.1.call-update
  476.7 1.9 gather_fusion.1
  478.6 132.5 %all-gather.5.cloned.1.call-done = bf16[256,8192]{1,0:T(8,128)(2,1)} async-done(((bf16[256,128]{1,0:T(8,128)(2,1)}), bf16[256,8192]{1,0:T(8,128)(2,1)}) %all-gather.5.cloned.1.call-update) | async-done | bytes 4194320 | tf_op jit(solution)/shard_map/all_gather | solution.py:43
  611.0 3.9 convolution_select_fusion
  614.9 276.2 %psum.15 = bf16[256,64]{0,1:T(8,128)(2,1)S(1)} all-reduce(f32[256,64]{0,1:T(8,128)S(1)} %convolution_select_fusion), channel_id=1, replica_groups=mesh['section'=8,'tensor'=64] {'tensor'}, use_global_device_ids=true, to_apply=%region_1.3 | all-reduce | flops 16384 | bytes 98304 | tf_op jit(solution)/shard_map/psum | solution.py:50
  891.1 0.0 copy-start.3
  891.1 0.1 broadcast_select_fusion
  891.3 0.0 copy-start.4
  891.3 0.8 fusion.11
  892.1 1.3 copy-done.3
  893.3 0.0 copy-done.4
  893.3 1.3 fusion.17
  894.6 0.7 pad_maximum_fusion
  (8 shorter events, 0.1 us)
Async XLA Ops:
  6.5 461.3 %copy-start = (bf16[1,8192,128]{2,1,0:T(8,128)(2,1)S(1)}, bf16[1,8192,128]{2,1,0:T(8,128)(2,1)}, u32[]{:S(2)}) copy-start(bf16[1,8192,128]{2,1,0:T(8,128)(2,1)} %param.13) | copy-start | bytes 6291460
  6.5 177.8 %all-gather.3.cloned.1.call-start = ((), (), s32[]{:S(2)}) async-start(), calls=%async_computation.1 | async-start | bytes 4259840 | tf_op jit(solution)/shard_map/all_gather | solution.py:43
  63.6 24.0 %copy-start.1 = (s32[64]{0:T(128)S(1)}, s32[64]{0:T(128)}, u32[]{:S(2)}) copy-start(s32[64]{0:T(128)} %param.12) | copy-start | bytes 772
  68.3 77.8 %all-to-all-start = ((bf16[64,2,4096]{2,1,0:T(2,128)(2,1)}), bf16[64,2,4096]{2,1,0:T(2,128)(2,1)S(1)}, u32[]{:S(2)}, u32[]{:S(2)}) async-start(bf16[64,2,4096]{2,1,0:T(2,128)(2,1)} %reshape.125), calls=%async_computation | async-start | bytes 2097152 | tf_op jit(solution)/shard_map/all_to_all | solution.py:31
  86.8 524.2 %all-gather.5.cloned.1.call-start = ((), (), s32[]{:S(2)}) async-start(), calls=%async_computation.2 | async-start | bytes 4259840 | tf_op jit(solution)/shard_map/all_gather | solution.py:43
  466.9 2.2 copy-start.2
  467.1 2.0 copy-start.5
  469.1 6.9 copy-start.6
  470.4 5.6 collective-permute-start
  891.1 2.2 copy-start.3
  891.3 2.0 copy-start.4
Sparse Core Ops, SparseCore 0:
  10.3 174.0 all-gather.2
  476.8 134.2 all-gather.4
where the time goes:
time: 903 us; the launch traced here: 902 us
  blocking collectives  555 us (61%)
  waiting for transfers between devices  215 us (24%)
  other arithmetic  48.2 us (5%)
  local copies, waits for them, and re-layouts  37.6 us (4%)
  starting transfers between devices  20.5 us (2%)
  between operations  13.6 us (2%)
  matrix products  11.9 us (1%)
    psum x2, blocking collectives, local(): chosen = lax.psum(mine, 'tensor').astype(jnp.bfloat16)  555 us
    all_gather x2, waiting for transfers between devices, local(): shard_part = lax.all_gather(current_state, 'tensor', axis=1, tiled=True)  154 us
    all_to_all x1, waiting for transfers between devices, local(): lax.all_to_all(adapter_up[0], 'tensor', split_axis=2, concat_axis=0, tile...  56.5 us
    unnamed x1, other arithmetic  46.6 us
    all_to_all x1, starting transfers between devices, local(): lax.all_to_all(adapter_up[0], 'tensor', split_axis=2, concat_axis=0, tile...  18.6 us
  transfers between devices with their start and end apart: 4, of which 4 were waited for; matrix products, arithmetic and copies ran while one was open for 9% of the time, Pallas kernels for 0%

commit v1 on v0

v1 whole, which is shorter than its diff:
```python
import functools

import jax
import jax.numpy as jnp
from jax import lax
from jax.experimental import pallas as pl
from jax.experimental.pallas import tpu as pltpu
from jax.sharding import PartitionSpec as P

TICKS = 2
CAP = 16
NX = 4
XFIRST = 96
MESH = pl.DeviceIdType.MESH
BF16, F32 = jnp.bfloat16, jnp.float32


def kernel(nz, hidden, arriving, ids, aslot, w_any, d_any, u_any, out, xa, xb, w, d, u, acc, pick, place, lsend, lrecv,
           ssem, rsem, lsem, lora_ssem, lora_rsem):
    nt = NX * nz
    half = nz // 2
    rows = out.shape[1]
    ra, rb = XFIRST, rows - XFIRST
    ha, hb = ra // 2, rb // 2
    rank = u.shape[0]
    section = lax.axis_index("section")
    sections = lax.axis_size("section")
    me = lax.axis_index("tensor")
    x, z = me // nz, me % nz
    x_next, x_back = ((x + 1) % NX) * nz + z, ((x + NX - 1) % NX) * nz + z
    z_next, z_back = x * nz + (z + 1) % nz, x * nz + (z + nz - 1) % nz
    s_next, s_back = (section + 1) % sections, (section + sections - 1) % sections
    x_to, z_to = (x_next, x_back), (z_next, z_back)

    locals_ = [
        pltpu.make_async_copy(hidden.at[0:ra], xa.at[0, 0, 0], lsem.at[0]),
        pltpu.make_async_copy(hidden.at[ra:rows], xb.at[0, 0, 0], lsem.at[1]),
        pltpu.make_async_copy(w_any, w, lsem.at[2]),
        pltpu.make_async_copy(d_any, d, lsem.at[3]),
        pltpu.make_async_copy(u_any, u, lsem.at[4]),
    ]
    entry = [
        pltpu.make_async_copy(arriving.at[0:ra], xa.at[1, 0, 0], lsem.at[5]),
        pltpu.make_async_copy(arriving.at[ra:rows], xb.at[1, 0, 0], lsem.at[6]),
    ]
    for c in locals_:
        c.start()

    @pl.when(section == 0)
    def _():
        for c in entry:
            c.start()

    barrier = pltpu.get_barrier_semaphore()
    for target in ((section, x_next), (section, x_back), (section, z_next), (section, z_back), (s_next, me), (s_back, me)):
        pl.semaphore_signal(barrier, inc=1, device_id=target, device_id_type=MESH)
    pl.semaphore_wait(barrier, 6)

    sent = []
    n = half + 1
    BZ, AZ, BX, BN, AX, AN, SH = 0, 2 * n, 6 * n, 8 * n, 10 * n, 10 * n + 2, 10 * n + 4

    def send(tick, sem, src, dst, to, where=None):
        c = pltpu.make_async_remote_copy(
            src_ref=src, dst_ref=dst, send_sem=ssem.at[tick, sem], recv_sem=rsem.at[tick, sem],
            device_id=(section, to) if where is None else where, device_id_type=MESH)
        c.start()
        sent.append(c)
        return c

    def slot_of(direction, k):
        return nz - 1 if k == half else 2 * k - 1 + direction

    def source(x_rel, slot):
        sx = (x + (0, NX - 1, 1, 2)[x_rel]) % NX
        if slot == 0:
            sz = z
        elif slot == nz - 1:
            sz = (z + half) % nz
        else:
            k = (slot + 1) // 2
            sz = (z + (nz - k if slot % 2 == 1 else k)) % nz
        return pl.multiple_of((sx * nz + sz) * 128, 128)

    def accumulate(first, count, chunks):
        lhs = jnp.concatenate([c for c, _ in chunks], axis=1)
        base = jnp.concatenate([w[pl.ds(o, 128), :] for _, o in chunks], axis=0)
        down = jnp.concatenate([d[:, pl.ds(o, 128)] for _, o in chunks], axis=1)
        acc[first:first + count, 0:128] += jnp.dot(lhs, base, preferred_element_type=F32)
        acc[first:first + count, 128:128 + rank] += lax.dot_general(lhs, down, (((1,), (1,)), ((), ())), preferred_element_type=F32)

    def compute_a(tick, slots):
        accumulate(0, ra, [(xa[tick, s, r], source(r, s)) for s in slots for r in range(NX)])

    def compute_b(tick, slots):
        accumulate(ra, rb, [(xb[tick, r, s], source(r, s)) for s in slots for r in range(NX)])

    def positions(tick):
        micro = jnp.where(section >= tick, section - tick, sections + tick - 1 - section)
        id_row = ids[micro].astype(F32)
        i0 = lax.broadcasted_iota(jnp.int32, (rows, rows), 0)
        i1 = lax.broadcasted_iota(jnp.int32, (rows, rows), 1)
        id_col = jnp.sum(jnp.where(i0 == i1, id_row, 0.0), axis=1, keepdims=True)
        same = id_col == id_row
        rank_row = jnp.sum(jnp.where(same & (i0 < i1), 1.0, 0.0), axis=0, keepdims=True)
        rank_col = jnp.sum(jnp.where(same & (i1 < i0), 1.0, 0.0), axis=1, keepdims=True)
        named = lax.broadcasted_iota(jnp.int32, (rows, nt), 1).astype(F32) == id_col
        slot_col = jnp.sum(jnp.where(named, aslot[...].astype(F32), 0.0), axis=1, keepdims=True)
        slot_row = jnp.sum(jnp.where(i0 == i1, slot_col, 0.0), axis=0, keepdims=True)
        j = lax.broadcasted_iota(jnp.int32, (CAP, rows), 0).astype(F32)
        pick[tick] = ((slot_row == me.astype(F32)) & (rank_row == j)).astype(BF16)
        q = lax.broadcasted_iota(jnp.int32, (rows, nt * CAP), 1).astype(F32)
        place[tick] = (slot_col * CAP + rank_col == q).astype(BF16)

    groups = ((0, 1), (1, 3))

    def tick_work(tick):
        bz, az, bx, bn = {}, {}, {}, {}
        acc[...] = jnp.zeros_like(acc)
        ax = [send(tick, AX + i, xa.at[tick, 0, 0], xa.at[tick, 0, 1 + i], x_to[i]) for i in (0, 1)]

        def send_bz(k):
            for i in (0, 1):
                s0, s1 = (0 if k == 1 else slot_of(i, k - 1)), slot_of(i, k)
                part = pl.ds(i * hb, hb) if k == half else pl.ds(0, rb)
                bz[i, k] = send(tick, BZ + i * n + k, xb.at[tick, 0, s0, part], xb.at[tick, 0, s1, part], z_to[i])

        def send_az(k, g):
            start, count = groups[g]
            for i in (0, 1):
                s0, s1 = (0 if k == 1 else slot_of(i, k - 1)), slot_of(i, k)
                if k == half:
                    start, count = 2 * i, 2
                part = pl.ds(start, count)
                az[i, k, g] = send(tick, AZ + (i * n + k) * 2 + g, xa.at[tick, s0, part], xa.at[tick, s1, part], z_to[i])

        def span(k):
            return pl.ds(0, 1) if k == 0 else pl.ds(nz - 1, 1) if k == half else pl.ds(2 * k - 1, 2)

        def slots(k):
            return (0,) if k == 0 else (nz - 1,) if k == half else (2 * k - 1, 2 * k)

        def send_bx(k):
            for i in (0, 1):
                bx[i, k] = send(tick, BX + i * n + k, xb.at[tick, 0, span(k)], xb.at[tick, 1 + i, span(k)], x_to[i])

        def send_bn(k):
            for i in (0, 1):
                bx[i, k].wait_recv()
            for i in (0, 1):
                if k in (0, half):
                    s, part = slots(k)[0], pl.ds(i * hb, hb)
                else:
                    s, part = slots(k)[i], pl.ds(0, rb)
                bn[i, k] = send(tick, BN + i * n + k, xb.at[tick, 1 + i, s, part], xb.at[tick, 3, s, part], x_to[i])

        def finish_b(k):
            for i in (0, 1):
                bn[i, k].wait_recv()
            compute_b(tick, slots(k))

        send_bz(1)
        send_az(1, 0)
        send_bx(0)
        if tick == 0:
            positions(0)
        for c in ax:
            c.wait_recv()
        an = [send(tick, AN + i, xa.at[tick, 0, 1 + i, pl.ds(i * ha, ha)], xa.at[tick, 0, 3, pl.ds(i * ha, ha)], x_to[i]) for i in (0, 1)]
        for c in an:
            c.wait_recv()
        send_az(1, 1)
        if tick == 0:
            positions(1)
            for c in locals_[2:]:
                c.wait()
        compute_a(tick, (0,))
        for k in range(1, half + 1):
            for i in (0, 1):
                bz[i, k].wait_recv()
            if k < half:
                send_bz(k + 1)
            send_bx(k)
            send_bn(k - 1)
            for g in ((0,) if k == half else (0, 1)):
                for i in (0, 1):
                    az[i, k, g].wait_recv()
                if k + 1 < half:
                    send_az(k + 1, g)
            if k + 1 == half:
                send_az(half, 0)
            compute_a(tick, slots(k))
            if k >= 2:
                finish_b(k - 2)
        send_bn(half)
        finish_b(half - 1)
        finish_b(half)

        low = jnp.dot(pick[tick], acc[:, 128:128 + rank].astype(BF16), preferred_element_type=F32).astype(BF16)
        wide = 512
        per = wide // 128

        def widen(i, carry):
            at = pl.multiple_of(i * wide, wide)
            part = jnp.dot(low, u[:, pl.ds(at, wide)], preferred_element_type=F32).astype(BF16)
            for j in range(per):
                lsend[i * per + j] = part[:, j * 128:(j + 1) * 128]
            return carry

        lax.fori_loop(0, nt // per, widen, 0)

        def spread(i, carry):
            to = (me + i) % nt
            pltpu.make_async_remote_copy(
                src_ref=lsend.at[to], dst_ref=lrecv.at[tick, me], send_sem=lora_ssem.at[tick], recv_sem=lora_rsem.at[tick],
                device_id=(section, to), device_id_type=MESH).start()
            return carry

        lax.fori_loop(1, nt, spread, 0)
        own = pltpu.make_async_copy(lsend.at[me], lrecv.at[tick, me], lsem.at[7])
        own.start()
        own.wait()
        others = pltpu.make_async_remote_copy(
            src_ref=lsend.at[0:nt - 1], dst_ref=lrecv.at[tick, 0:nt - 1], send_sem=lora_ssem.at[tick], recv_sem=lora_rsem.at[tick],
            device_id=(section, x_next), device_id_type=MESH)
        others.wait_recv()
        lora = jnp.dot(place[tick], lrecv[tick].reshape(nt * CAP, 128), preferred_element_type=F32)
        held = jnp.concatenate([xa[tick, 0, 0], xb[tick, 0, 0]], axis=0).astype(F32)
        out[tick] = (held + acc[:, 0:128] + lora).astype(BF16)
        others.wait_send()

    for c in locals_[:2]:
        c.wait()
    tick_work(0)

    shift = [
        pltpu.make_async_remote_copy(
            src_ref=out.at[0, first:first + count], dst_ref=dst, send_sem=ssem.at[0, SH + i], recv_sem=rsem.at[0, SH + i],
            device_id=(s_next, me), device_id_type=MESH)
        for i, (first, count, dst) in enumerate(((0, ra, xa.at[1, 0, 0]), (ra, rb, xb.at[1, 0, 0])))
    ]

    @pl.when(section + 1 < sections)
    def _():
        for c in shift:
            c.start()

    @pl.when(section > 0)
    def _():
        for c in shift:
            c.wait_recv()

    @pl.when(section == 0)
    def _():
        for c in entry:
            c.wait()

    tick_work(1)

    @pl.when(section + 1 < sections)
    def _():
        for c in shift:
            c.wait_send()

    for c in sent:
        c.wait_send()


def local(hidden, arriving, ids, adapter_slot, base_matrix, adapter_down, adapter_up):
    rows, cols = hidden.shape
    width = base_matrix.shape[1]
    rank = adapter_down.shape[3]
    nt = lax.axis_size("tensor")
    nz = nt // NX
    sems = 10 * (nz // 2 + 1) + 6
    vmem, hbm = pl.BlockSpec(memory_space=pltpu.VMEM), pl.BlockSpec(memory_space=pl.ANY)
    return pl.pallas_call(
        functools.partial(kernel, nz),
        out_shape=jax.ShapeDtypeStruct((TICKS, rows, cols), BF16),
        in_specs=[hbm, hbm, vmem, vmem, hbm, hbm, hbm],
        out_specs=vmem,
        scratch_shapes=[
            pltpu.VMEM((TICKS, nz, NX, XFIRST, cols), BF16),
            pltpu.VMEM((TICKS, NX, nz, rows - XFIRST, cols), BF16),
            pltpu.VMEM((width, cols), BF16),
            pltpu.VMEM((rank, width), BF16),
            pltpu.VMEM((rank, width), BF16),
            pltpu.VMEM((rows, cols + rank), F32),
            pltpu.VMEM((TICKS, CAP, rows), BF16),
            pltpu.VMEM((TICKS, rows, nt * CAP), BF16),
            pltpu.VMEM((nt, CAP, cols), BF16),
            pltpu.VMEM((TICKS, nt, CAP, cols), BF16),
            pltpu.SemaphoreType.DMA((TICKS, sems)),
            pltpu.SemaphoreType.DMA((TICKS, sems)),
            pltpu.SemaphoreType.DMA((8,)),
            pltpu.SemaphoreType.DMA((TICKS,)),
            pltpu.SemaphoreType.DMA((TICKS,)),
        ],
        compiler_params=pltpu.CompilerParams(collective_id=0, has_side_effects=True, vmem_limit_bytes=40 * 1024 * 1024),
    )(hidden, arriving, ids.reshape(ids.shape[0], 1, ids.shape[1]), adapter_slot.reshape(1, nt), base_matrix[0], adapter_down[0, 0].T, adapter_up[0, 0])


def solution(mesh):
    in_specs = (
        P("section", "tensor"),
        P(None, "tensor"),
        P(),
        P(),
        P("section", None, "tensor"),
        P("section", "tensor", None, None),
        P("section", "tensor", None, None),
    )
    out_specs = P(None, "section", "tensor")
    return jax.shard_map(local, mesh=mesh, in_specs=in_specs, out_specs=out_specs, check_vma=False)
```

time: 903 us -> 143 us (0.16)
  the two profiles are of different devices: /device:TPU:8 before, /device:TPU:2 now
where the time goes in v1:
time: 143 us
  Pallas kernels  135 us (94%)
  local copies, waits for them, and re-layouts  7.73 us (5%)
    pallas_call x1, Pallas kernels, local(): pl.pallas_call(functools.partial(kernel, nz), out_shape=jax.ShapeDtypeStr...  135 us
    unnamed x15, local copies, waits for them, and re-layouts  7.73 us

profile of v1, /device:TPU:2, one launch (start us, length us, event | category | flops | bytes accessed | tf_op | source)
XLA Modules:
  0.0 142.8 jit_solution(4751638289978772501)
XLA Ops:
  0.0 0.0 copy-start
  0.0 1.6 %copy-done = bf16[1,8192,128]{2,1,0:T(8,128)(2,1)S(1)} copy-done((bf16[1,8192,128]{2,1,0:T(8,128)(2,1)S(1)}, bf16[1,8192,128]{2,1,0:T(8,128)(2,1)}, u32[]{:S(2)}) %copy-start) | copy-done | bytes 2097176
  1.6 0.0 copy-start.1
  1.6 1.2 copy-done.1
  2.8 0.0 copy-start.2
  2.8 1.2 copy-done.2
  4.0 0.0 copy-start.3
  4.0 0.8 copy-done.3
  4.9 0.0 copy-start.4
  4.9 0.8 copy-done.4
  5.7 0.0 copy-start.5
  5.7 0.7 copy-done.5
  6.4 0.0 copy-start.6
  6.4 0.7 copy-done.6
  7.1 135.1 %shard_map.73 = bf16[2,256,128]{2,1,0:T(8,128)(2,1)S(1)} custom-call(bf16[256,128]{1,0:T(8,128)(2,1)S(1)} %copy-done.3, bf16[256,128]{1,0:T(8,128)(2,1)S(1)} %copy-done.4, s32[9,1,256]{2,1,0:T(1,128)S(1)} %bitcast.10, s32[1,64]{1,0:T(1,128)S(1)} %bitcast.11, bf16[8192,128]{1,0:T(8,128)(2,1)S(1)} %bitcast.7, bf16[64,8192]{1,0:T(8,128)(2,1)S(1)} %bitcast.8, ...), custom_call_target="tpu_custom_call" | custom-call | tf_op jit(solution)/shard_map/pallas_call | solution.py:277
  142.2 0.7 copy.9
Async XLA Ops:
  0.0 1.6 %copy-start = (bf16[1,8192,128]{2,1,0:T(8,128)(2,1)S(1)}, bf16[1,8192,128]{2,1,0:T(8,128)(2,1)}, u32[]{:S(2)}) copy-start(bf16[1,8192,128]{2,1,0:T(8,128)(2,1)} %param.11) | copy-start | bytes 6291460
  1.6 1.2 copy-start.1
  2.8 1.2 copy-start.2
  4.0 0.8 copy-start.3
  4.9 0.8 copy-start.4
  5.7 0.7 copy-start.5
  6.4 0.7 copy-start.6

commit v2 on v1

v2 whole, which is shorter than its diff:
```python
import functools

import jax
import jax.numpy as jnp
from jax import lax
from jax.experimental import pallas as pl
from jax.experimental.pallas import tpu as pltpu
from jax.sharding import PartitionSpec as P

TICKS = 2
CAP = 16
NX = 4
B_ROWS = 128
MESH = pl.DeviceIdType.MESH
BF16, F32 = jnp.bfloat16, jnp.float32


def kernel(nz, hidden, arriving, ids, aslot, w_any, d_any, u_any, out, xb, xc, w, d, u, acc, pick, place, lsend, lrecv,
           ssem, rsem, lsem, lora_ssem, lora_rsem):
    nt = NX * nz
    half = nz // 2
    rows = out.shape[1]
    rb, rc = B_ROWS, rows - B_ROWS
    hb, hc = rb // 2, rc // 2
    rank = u.shape[0]
    section = lax.axis_index("section")
    sections = lax.axis_size("section")
    me = lax.axis_index("tensor")
    x, z = me // nz, me % nz
    x_next, x_back = ((x + 1) % NX) * nz + z, ((x + NX - 1) % NX) * nz + z
    z_next, z_back = x * nz + (z + 1) % nz, x * nz + (z + nz - 1) % nz
    s_next, s_back = (section + 1) % sections, (section + sections - 1) % sections
    x_to, z_to = (x_next, x_back), (z_next, z_back)
    z_jump = x * nz + (z + 2) % nz, x * nz + (z + nz - 2) % nz

    locals_ = [
        pltpu.make_async_copy(hidden.at[0:rb], xb.at[0, 0, 0], lsem.at[0]),
        pltpu.make_async_copy(hidden.at[rb:rows], xc.at[0, 0, 0], lsem.at[1]),
        pltpu.make_async_copy(w_any, w, lsem.at[2]),
        pltpu.make_async_copy(d_any, d, lsem.at[3]),
        pltpu.make_async_copy(u_any, u, lsem.at[4]),
    ]
    entry = [
        pltpu.make_async_copy(arriving.at[0:rb], xb.at[1, 0, 0], lsem.at[5]),
        pltpu.make_async_copy(arriving.at[rb:rows], xc.at[1, 0, 0], lsem.at[6]),
    ]
    for c in locals_:
        c.start()

    @pl.when(section == 0)
    def _():
        for c in entry:
            c.start()

    barrier = pltpu.get_barrier_semaphore()
    near = [(section, t) for t in x_to + z_to + z_jump] + [(s_next, me), (s_back, me)]
    for target in near:
        pl.semaphore_signal(barrier, inc=1, device_id=target, device_id_type=MESH)
    pl.semaphore_wait(barrier, len(near))

    sent = []
    stages = half // 2
    n = stages + 1
    EB, EC, FB, FC, XB, XC, NB, NC, SH = (2 * n * i for i in range(9))

    def send(tick, sem, src, dst, to):
        c = pltpu.make_async_remote_copy(
            src_ref=src, dst_ref=dst, send_sem=ssem.at[tick, sem], recv_sem=rsem.at[tick, sem],
            device_id=(section, to), device_id_type=MESH)
        c.start()
        sent.append(c)
        return c

    b_offsets = [0]
    for s in range(stages):
        b_offsets += [2 * s + 1, 2 * s + 2, -2 * s - 1] + ([-2 * s - 2] if s + 1 < stages else [])
    c_offsets = [0]
    for s in range(1, stages):
        c_offsets += [2 * s, -2 * s]
    c_offsets += [half]
    for s in range(stages):
        c_offsets += [2 * s + 1, -2 * s - 1]

    def slot_at(offsets, direction, distance):
        return offsets.index(distance if direction == 0 or distance in (0, half) else -distance)

    def source(x_rel, offset):
        sx = (x + (0, NX - 1, 1, 2)[x_rel]) % NX
        sz = (z + nz - offset) % nz
        return pl.multiple_of((sx * nz + sz) * 128, 128)

    def accumulate(first, count, chunks):
        lhs = jnp.concatenate([c for c, _ in chunks], axis=1)
        base = jnp.concatenate([w[pl.ds(o, 128), :] for _, o in chunks], axis=0)
        down = jnp.concatenate([d[:, pl.ds(o, 128)] for _, o in chunks], axis=1)
        acc[first:first + count, 0:128] += jnp.dot(lhs, base, preferred_element_type=F32)
        acc[first:first + count, 128:128 + rank] += lax.dot_general(lhs, down, (((1,), (1,)), ((), ())), preferred_element_type=F32)

    def compute_b(tick, slots):
        accumulate(0, rb, [(xb[tick, r, s], source(r, b_offsets[s])) for s in slots for r in range(NX)])

    def compute_c(tick, slots):
        accumulate(rb, rc, [(xc[tick, s, r], source(r, c_offsets[s])) for s in slots for r in range(NX)])

    def positions(tick):
        micro = jnp.where(section >= tick, section - tick, sections + tick - 1 - section)
        id_row = ids[micro].astype(F32)
        i0 = lax.broadcasted_iota(jnp.int32, (rows, rows), 0)
        i1 = lax.broadcasted_iota(jnp.int32, (rows, rows), 1)
        id_col = jnp.sum(jnp.where(i0 == i1, id_row, 0.0), axis=1, keepdims=True)
        same = id_col == id_row
        rank_row = jnp.sum(jnp.where(same & (i0 < i1), 1.0, 0.0), axis=0, keepdims=True)
        rank_col = jnp.sum(jnp.where(same & (i1 < i0), 1.0, 0.0), axis=1, keepdims=True)
        named = lax.broadcasted_iota(jnp.int32, (rows, nt), 1).astype(F32) == id_col
        slot_col = jnp.sum(jnp.where(named, aslot[...].astype(F32), 0.0), axis=1, keepdims=True)
        slot_row = jnp.sum(jnp.where(i0 == i1, slot_col, 0.0), axis=0, keepdims=True)
        j = lax.broadcasted_iota(jnp.int32, (CAP, rows), 0).astype(F32)
        pick[tick] = ((slot_row == me.astype(F32)) & (rank_row == j)).astype(BF16)
        q = lax.broadcasted_iota(jnp.int32, (rows, nt * CAP), 1).astype(F32)
        place[tick] = (slot_col * CAP + rank_col == q).astype(BF16)

    def b_group(s):
        return (0, 1) if s == 0 else (4 * s - 3, 4 if s < stages else 3)

    def c_group(s):
        return (0, 1) if s == 0 else (2 * s - 1, 2 if s < stages else 1)

    def tick_work(tick):
        eb, ec, fb, fc, bx, cx, bn, cn = {}, {}, {}, {}, {}, {}, {}, {}

        def express(s):
            for i in (0, 1):
                s0, s1 = slot_at(b_offsets, i, 2 * s), slot_at(b_offsets, i, 2 * s + 2)
                part = pl.ds(i * hb, hb) if s + 1 == stages else pl.ds(0, rb)
                eb[i, s + 1] = send(tick, EB + 2 * s + i, xb.at[tick, 0, s0, part], xb.at[tick, 0, s1, part], z_jump[i])
            for i in (0, 1):
                s0, s1 = slot_at(c_offsets, i, 2 * s), slot_at(c_offsets, i, 2 * s + 2)
                part = pl.ds(i * hc, hc) if s + 1 == stages else pl.ds(0, rc)
                ec[i, s + 1] = send(tick, EC + 2 * s + i, xc.at[tick, s0, 0, part], xc.at[tick, s1, 0, part], z_jump[i])

        def fill_b(s):
            for i in (0, 1):
                s0, s1 = slot_at(b_offsets, i, 2 * s), slot_at(b_offsets, i, 2 * s + 1)
                fb[i, s] = send(tick, FB + 2 * s + i, xb.at[tick, 0, s0], xb.at[tick, 0, s1], z_to[i])

        def fill_c(s):
            for i in (0, 1):
                cn[i, s].wait_recv()
            for i in (0, 1):
                s0, s1 = slot_at(c_offsets, i, 2 * s), slot_at(c_offsets, i, 2 * s + 1)
                fc[i, s] = send(tick, FC + 2 * s + i, xc.at[tick, s0], xc.at[tick, s1], z_to[i])

        def x_b(s):
            part = pl.ds(*b_group(s))
            for i in (0, 1):
                bx[i, s] = send(tick, XB + 2 * s + i, xb.at[tick, 0, part], xb.at[tick, 1 + i, part], x_to[i])

        def x_c(s):
            part = pl.ds(*c_group(s))
            for i in (0, 1):
                cx[i, s] = send(tick, XC + 2 * s + i, xc.at[tick, part, 0], xc.at[tick, part, 1 + i], x_to[i])

        def across_b(s):
            first, count = b_group(s)
            for i in (0, 1):
                bx[i, s].wait_recv()
                if count == 4:
                    part, lines = pl.ds(first + 2 * i, 2), pl.ds(0, rb)
                else:
                    part, lines = pl.ds(first, count), pl.ds(i * hb, hb)
                bn[i, s] = send(tick, NB + 2 * s + i, xb.at[tick, 1 + i, part, lines], xb.at[tick, 3, part, lines], x_to[i])

        def across_c(s):
            first, count = c_group(s)
            for i in (0, 1):
                cx[i, s].wait_recv()
                if count == 2:
                    part, lines = pl.ds(first + i, 1), pl.ds(0, rc)
                else:
                    part, lines = pl.ds(first, 1), pl.ds(i * hc, hc)
                cn[i, s] = send(tick, NC + 2 * s + i, xc.at[tick, part, 1 + i, lines], xc.at[tick, part, 3, lines], x_to[i])

        def arrived(copies, s):
            for i in (0, 1):
                copies[i, s].wait_recv()

        def finish_b(s):
            arrived(bn, s)
            first, count = b_group(s)
            compute_b(tick, range(first, first + count))

        def finish_c(s):
            first, count = c_group(s)
            compute_c(tick, range(first, first + count))

        def finish_odd(s):
            arrived(fc, s)
            compute_c(tick, [slot_at(c_offsets, i, 2 * s + 1) for i in (0, 1)])

        express(0)
        x_c(0)
        fill_b(0)
        x_b(0)
        acc[...] = jnp.zeros_like(acc)
        if tick == 0:
            positions(0)
        across_c(0)
        across_b(0)
        for s in range(1, stages):
            arrived(eb, s)
            arrived(ec, s)
            express(s)
            x_c(s)
            fill_b(s)
            arrived(fb, s - 1)
            x_b(s)
            fill_c(s - 1)
            if tick == 0 and s == 1:
                positions(1)
                for c in locals_[2:]:
                    c.wait()
            finish_c(s - 1)
            finish_b(s - 1)
            across_c(s)
            across_b(s)
            if s > 1:
                finish_odd(s - 2)
        if tick == 0 and stages == 1:
            positions(1)
            for c in locals_[2:]:
                c.wait()
        arrived(eb, stages)
        arrived(ec, stages)
        x_c(stages)
        arrived(fb, stages - 1)
        x_b(stages)
        fill_c(stages - 1)
        finish_c(stages - 1)
        finish_b(stages - 1)
        across_c(stages)
        across_b(stages)
        if stages > 1:
            finish_odd(stages - 2)
        arrived(cn, stages)
        finish_c(stages)
        finish_odd(stages - 1)
        finish_b(stages)

        low = jnp.dot(pick[tick], acc[:, 128:128 + rank].astype(BF16), preferred_element_type=F32).astype(BF16)
        for dx in (2, 1, 3, 0):
            first = ((x + dx) % NX) * nz
            at = pl.multiple_of(first * 128, 128)
            part = jnp.dot(low, u[:, pl.ds(at, nz * 128)], preferred_element_type=F32).astype(BF16)
            for j in range(nz):
                lsend[first + j] = part[:, j * 128:(j + 1) * 128]

            def spread(i, carry):
                dz = (half + (1 - 2 * (i % 2)) * ((i + 1) // 2)) % nz
                to = first + (z + dz) % nz
                pltpu.make_async_remote_copy(
                    src_ref=lsend.at[to], dst_ref=lrecv.at[tick, me], send_sem=lora_ssem.at[tick], recv_sem=lora_rsem.at[tick],
                    device_id=(section, to), device_id_type=MESH).start()
                return carry

            lax.fori_loop(0, nz if dx else nz - 1, spread, 0)
        own = pltpu.make_async_copy(lsend.at[me], lrecv.at[tick, me], lsem.at[7])
        own.start()
        own.wait()
        others = pltpu.make_async_remote_copy(
            src_ref=lsend.at[0:nt - 1], dst_ref=lrecv.at[tick, 0:nt - 1], send_sem=lora_ssem.at[tick], recv_sem=lora_rsem.at[tick],
            device_id=(section, x_next), device_id_type=MESH)
        others.wait_recv()
        lora = jnp.dot(place[tick], lrecv[tick].reshape(nt * CAP, 128), preferred_element_type=F32)
        held = jnp.concatenate([xb[tick, 0, 0], xc[tick, 0, 0]], axis=0).astype(F32)
        out[tick] = (held + acc[:, 0:128] + lora).astype(BF16)
        others.wait_send()

    for c in locals_[:2]:
        c.wait()
    tick_work(0)

    shift = [
        pltpu.make_async_remote_copy(
            src_ref=out.at[0, first:first + count], dst_ref=dst, send_sem=ssem.at[0, SH + i], recv_sem=rsem.at[0, SH + i],
            device_id=(s_next, me), device_id_type=MESH)
        for i, (first, count, dst) in enumerate(((0, rb, xb.at[1, 0, 0]), (rb, rc, xc.at[1, 0, 0])))
    ]

    @pl.when(section + 1 < sections)
    def _():
        for c in shift:
            c.start()

    @pl.when(section > 0)
    def _():
        for c in shift:
            c.wait_recv()

    @pl.when(section == 0)
    def _():
        for c in entry:
            c.wait()

    tick_work(1)

    @pl.when(section + 1 < sections)
    def _():
        for c in shift:
            c.wait_send()

    for c in sent:
        c.wait_send()


def local(hidden, arriving, ids, adapter_slot, base_matrix, adapter_down, adapter_up):
    rows, cols = hidden.shape
    width = base_matrix.shape[1]
    rank = adapter_down.shape[3]
    nt = lax.axis_size("tensor")
    nz = nt // NX
    sems = 16 * (nz // 4 + 1) + 2
    vmem, hbm = pl.BlockSpec(memory_space=pltpu.VMEM), pl.BlockSpec(memory_space=pl.ANY)
    return pl.pallas_call(
        functools.partial(kernel, nz),
        out_shape=jax.ShapeDtypeStruct((TICKS, rows, cols), BF16),
        in_specs=[hbm, hbm, vmem, vmem, hbm, hbm, hbm],
        out_specs=vmem,
        scratch_shapes=[
            pltpu.VMEM((TICKS, NX, nz, B_ROWS, cols), BF16),
            pltpu.VMEM((TICKS, nz, NX, rows - B_ROWS, cols), BF16),
            pltpu.VMEM((width, cols), BF16),
            pltpu.VMEM((rank, width), BF16),
            pltpu.VMEM((rank, width), BF16),
            pltpu.VMEM((rows, cols + rank), F32),
            pltpu.VMEM((TICKS, CAP, rows), BF16),
            pltpu.VMEM((TICKS, rows, nt * CAP), BF16),
            pltpu.VMEM((nt, CAP, cols), BF16),
            pltpu.VMEM((TICKS, nt, CAP, cols), BF16),
            pltpu.SemaphoreType.DMA((TICKS, sems)),
            pltpu.SemaphoreType.DMA((TICKS, sems)),
            pltpu.SemaphoreType.DMA((8,)),
            pltpu.SemaphoreType.DMA((TICKS,)),
            pltpu.SemaphoreType.DMA((TICKS,)),
        ],
        compiler_params=pltpu.CompilerParams(collective_id=0, has_side_effects=True, vmem_limit_bytes=60 * 1024 * 1024),
    )(hidden, arriving, ids.reshape(ids.shape[0], 1, ids.shape[1]), adapter_slot.reshape(1, nt), base_matrix[0], adapter_down[0, 0].T, adapter_up[0, 0])


def solution(mesh):
    in_specs = (
        P("section", "tensor"),
        P(None, "tensor"),
        P(),
        P(),
        P("section", None, "tensor"),
        P("section", "tensor", None, None),
        P("section", "tensor", None, None),
    )
    out_specs = P(None, "section", "tensor")
    return jax.shard_map(local, mesh=mesh, in_specs=in_specs, out_specs=out_specs, check_vma=False)
```

time: 143 us -> 119 us (0.83)
  the two profiles are of different devices: /device:TPU:2 before, /device:TPU:8 now
where the time goes in v2:
time: 119 us
  Pallas kernels  118 us (99%)
  local copies, waits for them, and re-layouts  1.57 us (1%)
    pallas_call x1, Pallas kernels, local(): pl.pallas_call(functools.partial(kernel, nz), out_shape=jax.ShapeDtypeStr...  118 us

profile of v2, /device:TPU:8, one launch (start us, length us, event | category | flops | bytes accessed | tf_op | source)
XLA Modules:
  0.0 119.2 jit_solution(11519264598660171752)
XLA Ops:
  0.0 117.6 %shard_map.73 = bf16[2,256,128]{2,1,0:T(8,128)(2,1)} custom-call(bf16[256,128]{1,0:T(8,128)(2,1)} %hidden.1, bf16[256,128]{1,0:T(8,128)(2,1)} %arriving.1, s32[9,1,256]{2,1,0:T(1,128)} %bitcast.10, s32[1,64]{1,0:T(1,128)} %bitcast.11, bf16[8192,128]{1,0:T(8,128)(2,1)} %bitcast.7, bf16[64,8192]{1,0:T(8,128)(2,1)} %bitcast.8, bf16[64,8192]{1,0:T(8,128)(2,1)} %bitcast.9), custom_call_target="tpu_custom_call" | custom-call | tf_op jit(solution)/shard_map/pallas_call | solution.py:323
  117.6 1.6 %copy.9 = bf16[2,256,128]{2,1,0:T(8,128)(2,1)} copy(bf16[2,256,128]{2,1,0:T(8,128)(2,1)} %shard_map.73) | data formatting | bytes 262144

commit v3 on v2

--- a/solution.py
+++ b/solution.py
@@ -10,7 +10,13 @@
 TICKS = 2
 CAP = 16
 NX = 4
-B_ROWS = 128
+B_ROWS = 96
+ORDER = (
+    "CE0", "CX0", "BE0", "BP0", "BX0", "CA0", "CE1", "CX1", "BA0", "BE1", "BP1", "BX1", "CF0", "CK0", "CE2", "CX2",
+    "CA1", "BK0", "BE2", "BP2", "BX2", "BA1", "CA2", "CG0", "CF1", "CK1", "CE3", "CX3", "BA2", "BE3", "BP3", "BX3",
+    "BK1", "CF2", "CK2", "CA3", "CG1", "BK2", "CE4", "CX4", "BE4", "BX4", "BA3", "CF3", "CK3", "CA4", "CG2", "BA4",
+    "BK3", "CK4", "CG3", "BK4",
+)
 MESH = pl.DeviceIdType.MESH
 BF16, F32 = jnp.bfloat16, jnp.float32
 
@@ -53,22 +59,39 @@
             c.start()
 
     barrier = pltpu.get_barrier_semaphore()
-    near = [(section, t) for t in x_to + z_to + z_jump] + [(s_next, me), (s_back, me)]
-    for target in near:
+    senders = [(section, t) for t in x_to + z_to + z_jump] + [(s_back, me)]
+    for target in senders:
         pl.semaphore_signal(barrier, inc=1, device_id=target, device_id_type=MESH)
-    pl.semaphore_wait(barrier, len(near))
+    pl.semaphore_wait(barrier, len(senders))
 
     sent = []
     stages = half // 2
     n = stages + 1
     EB, EC, FB, FC, XB, XC, NB, NC, SH = (2 * n * i for i in range(9))
-
-    def send(tick, sem, src, dst, to):
+    later = []
+
+    def send(tick, sem, src, dst, to, first_line=None):
         c = pltpu.make_async_remote_copy(
             src_ref=src, dst_ref=dst, send_sem=ssem.at[tick, sem], recv_sem=rsem.at[tick, sem],
             device_id=(section, to), device_id_type=MESH)
-        c.start()
-        sent.append(c)
+        if tick == 0 or first_line is None:
+            c.start()
+            sent.append(c)
+            return c
+        lines = src.shape[-2]
+        ahead = pltpu.make_async_remote_copy(
+            src_ref=out.at[tick - 1, first_line:first_line + lines], dst_ref=dst, send_sem=ssem.at[tick - 1, SH + 2 + len(later) // 2],
+            recv_sem=rsem.at[tick, sem], device_id=(s_next, to), device_id_type=MESH)
+
+        @pl.when(section + 1 < sections)
+        def _():
+            ahead.start()
+
+        @pl.when(section == 0)
+        def _():
+            c.start()
+
+        later.extend([(section + 1 < sections, ahead), (section == 0, c)])
         return c
 
     b_offsets = [0]
@@ -128,37 +151,46 @@
     def tick_work(tick):
         eb, ec, fb, fc, bx, cx, bn, cn = {}, {}, {}, {}, {}, {}, {}, {}
 
-        def express(s):
-            for i in (0, 1):
+        def express_b(s):
+            if s > 0:
+                arrived(eb, s)
+            for i in (0, 1) if s < stages else ():
                 s0, s1 = slot_at(b_offsets, i, 2 * s), slot_at(b_offsets, i, 2 * s + 2)
                 part = pl.ds(i * hb, hb) if s + 1 == stages else pl.ds(0, rb)
-                eb[i, s + 1] = send(tick, EB + 2 * s + i, xb.at[tick, 0, s0, part], xb.at[tick, 0, s1, part], z_jump[i])
-            for i in (0, 1):
+                eb[i, s + 1] = send(tick, EB + 2 * s + i, xb.at[tick, 0, s0, part], xb.at[tick, 0, s1, part], z_jump[i],
+                                    first_line=None if s else i * hb if s + 1 == stages else 0)
+
+        def express_c(s):
+            if s > 0:
+                arrived(ec, s)
+            for i in (0, 1) if s < stages else ():
                 s0, s1 = slot_at(c_offsets, i, 2 * s), slot_at(c_offsets, i, 2 * s + 2)
                 part = pl.ds(i * hc, hc) if s + 1 == stages else pl.ds(0, rc)
-                ec[i, s + 1] = send(tick, EC + 2 * s + i, xc.at[tick, s0, 0, part], xc.at[tick, s1, 0, part], z_jump[i])
+                ec[i, s + 1] = send(tick, EC + 2 * s + i, xc.at[tick, s0, 0, part], xc.at[tick, s1, 0, part], z_jump[i],
+                                    first_line=None if s else rb + (i * hc if s + 1 == stages else 0))
 
         def fill_b(s):
             for i in (0, 1):
                 s0, s1 = slot_at(b_offsets, i, 2 * s), slot_at(b_offsets, i, 2 * s + 1)
-                fb[i, s] = send(tick, FB + 2 * s + i, xb.at[tick, 0, s0], xb.at[tick, 0, s1], z_to[i])
+                fb[i, s] = send(tick, FB + 2 * s + i, xb.at[tick, 0, s0], xb.at[tick, 0, s1], z_to[i], first_line=None if s else 0)
 
         def fill_c(s):
-            for i in (0, 1):
-                cn[i, s].wait_recv()
+            arrived(cn, s)
             for i in (0, 1):
                 s0, s1 = slot_at(c_offsets, i, 2 * s), slot_at(c_offsets, i, 2 * s + 1)
                 fc[i, s] = send(tick, FC + 2 * s + i, xc.at[tick, s0], xc.at[tick, s1], z_to[i])
 
         def x_b(s):
-            part = pl.ds(*b_group(s))
-            for i in (0, 1):
-                bx[i, s] = send(tick, XB + 2 * s + i, xb.at[tick, 0, part], xb.at[tick, 1 + i, part], x_to[i])
+            if s > 0:
+                arrived(fb, s - 1)
+            part = pl.ds(*b_group(s)) if s else 0
+            for i in (0, 1):
+                bx[i, s] = send(tick, XB + 2 * s + i, xb.at[tick, 0, part], xb.at[tick, 1 + i, part], x_to[i], first_line=None if s else 0)
 
         def x_c(s):
-            part = pl.ds(*c_group(s))
-            for i in (0, 1):
-                cx[i, s] = send(tick, XC + 2 * s + i, xc.at[tick, part, 0], xc.at[tick, part, 1 + i], x_to[i])
+            part = pl.ds(*c_group(s)) if s else 0
+            for i in (0, 1):
+                cx[i, s] = send(tick, XC + 2 * s + i, xc.at[tick, part, 0], xc.at[tick, part, 1 + i], x_to[i], first_line=None if s else rb)
 
         def across_b(s):
             first, count = b_group(s)
@@ -190,6 +222,8 @@
             compute_b(tick, range(first, first + count))
 
         def finish_c(s):
+            if s == stages:
+                arrived(cn, s)
             first, count = c_group(s)
             compute_c(tick, range(first, first + count))
 
@@ -197,54 +231,33 @@
             arrived(fc, s)
             compute_c(tick, [slot_at(c_offsets, i, 2 * s + 1) for i in (0, 1)])
 
-        express(0)
-        x_c(0)
-        fill_b(0)
-        x_b(0)
+        tasks = dict(BE=express_b, BP=fill_b, BX=x_b, BA=across_b, BK=finish_b, CE=express_c, CX=x_c, CA=across_c, CF=fill_c, CK=finish_c,
+                     CG=finish_odd)
+        if stages == 4:
+            steps = ORDER
+        else:
+            steps = [k + str(s) for s in range(stages) for k in ("CE", "CX", "BE", "BP", "BX", "CA", "CF", "BA", "CK", "BK")]
+            steps += [k + str(stages) for k in ("CE", "CX", "BE", "BX", "CA", "CK", "BA", "BK")]
+            steps += ["CG" + str(s) for s in range(stages)]
         acc[...] = jnp.zeros_like(acc)
-        if tick == 0:
-            positions(0)
-        across_c(0)
-        across_b(0)
-        for s in range(1, stages):
-            arrived(eb, s)
-            arrived(ec, s)
-            express(s)
-            x_c(s)
-            fill_b(s)
-            arrived(fb, s - 1)
-            x_b(s)
-            fill_c(s - 1)
-            if tick == 0 and s == 1:
-                positions(1)
-                for c in locals_[2:]:
-                    c.wait()
-            finish_c(s - 1)
-            finish_b(s - 1)
-            across_c(s)
-            across_b(s)
-            if s > 1:
-                finish_odd(s - 2)
-        if tick == 0 and stages == 1:
-            positions(1)
-            for c in locals_[2:]:
-                c.wait()
-        arrived(eb, stages)
-        arrived(ec, stages)
-        x_c(stages)
-        arrived(fb, stages - 1)
-        x_b(stages)
-        fill_c(stages - 1)
-        finish_c(stages - 1)
-        finish_b(stages - 1)
-        across_c(stages)
-        across_b(stages)
-        if stages > 1:
-            finish_odd(stages - 2)
-        arrived(cn, stages)
-        finish_c(stages)
-        finish_odd(stages - 1)
-        finish_b(stages)
+        loaded = False
+        for at, step in enumerate(steps):
+            if tick == 0 and at == 5:
+                positions(0)
+            if not loaded and step[1] in "FKG":
+                if tick == 0:
+                    for c in locals_[2:]:
+                        c.wait()
+                    positions(1)
+                else:
+                    entered()
+                loaded = True
+            tasks[step[:2]](int(step[2:]))
+            if tick == 1 and at == 4:
+                @pl.when(section + 1 < sections)
+                def _():
+                    for c in shift:
+                        c.start()
 
         low = jnp.dot(pick[tick], acc[:, 128:128 + rank].astype(BF16), preferred_element_type=F32).astype(BF16)
         for dx in (2, 1, 3, 0):
@@ -275,10 +288,6 @@
         out[tick] = (held + acc[:, 0:128] + lora).astype(BF16)
         others.wait_send()
 
-    for c in locals_[:2]:
-        c.wait()
-    tick_work(0)
-
     shift = [
         pltpu.make_async_remote_copy(
             src_ref=out.at[0, first:first + count], dst_ref=dst, send_sem=ssem.at[0, SH + i], recv_sem=rsem.at[0, SH + i],
@@ -286,15 +295,15 @@
         for i, (first, count, dst) in enumerate(((0, rb, xb.at[1, 0, 0]), (rb, rc, xc.at[1, 0, 0])))
     ]
 
-    @pl.when(section + 1 < sections)
-    def _():
-        for c in shift:
-            c.start()
-
-    @pl.when(section > 0)
-    def _():
-        for c in shift:
-            c.wait_recv()
+    def entered():
+        @pl.when(section > 0)
+        def _():
+            for c in shift:
+                c.wait_recv()
+
+    for c in locals_[:2]:
+        c.wait()
+    tick_work(0)
 
     @pl.when(section == 0)
     def _():
@@ -310,6 +319,10 @@
 
     for c in sent:
         c.wait_send()
+    for some, c in later:
+        @pl.when(some)
+        def _():
+            c.wait_send()
 
 
 def local(hidden, arriving, ids, adapter_slot, base_matrix, adapter_down, adapter_up):
@@ -318,7 +331,7 @@
     rank = adapter_down.shape[3]
     nt = lax.axis_size("tensor")
     nz = nt // NX
-    sems = 16 * (nz // 4 + 1) + 2
+    sems = 16 * (nz // 4 + 1) + 12
     vmem, hbm = pl.BlockSpec(memory_space=pltpu.VMEM), pl.BlockSpec(memory_space=pl.ANY)
     return pl.pallas_call(
         functools.partial(kernel, nz),

time: 119 us -> 108 us (0.908)
  the two profiles are of different devices: /device:TPU:8 before, /device:TPU:32 now
where the time goes in v3:
time: 108 us
  Pallas kernels  107 us (99%)
  local copies, waits for them, and re-layouts  1.57 us (1%)
    pallas_call x1, Pallas kernels, local(): pl.pallas_call(functools.partial(kernel, nz), out_shape=jax.ShapeDtypeStr...  107 us

profile of v3, /device:TPU:32, one launch (start us, length us, event | category | flops | bytes accessed | tf_op | source)
XLA Modules:
  0.0 108.3 jit_solution(4368762429769060216)
XLA Ops:
  0.0 106.7 %shard_map.73 = bf16[2,256,128]{2,1,0:T(8,128)(2,1)} custom-call(bf16[256,128]{1,0:T(8,128)(2,1)} %hidden.1, bf16[256,128]{1,0:T(8,128)(2,1)} %arriving.1, s32[9,1,256]{2,1,0:T(1,128)} %bitcast.10, s32[1,64]{1,0:T(1,128)} %bitcast.11, bf16[8192,128]{1,0:T(8,128)(2,1)} %bitcast.7, bf16[64,8192]{1,0:T(8,128)(2,1)} %bitcast.8, bf16[64,8192]{1,0:T(8,128)(2,1)} %bitcast.9), custom_call_target="tpu_custom_call" | custom-call | tf_op jit(solution)/shard_map/pallas_call | solution.py:336
  106.7 1.6 %copy.9 = bf16[2,256,128]{2,1,0:T(8,128)(2,1)} copy(bf16[2,256,128]{2,1,0:T(8,128)(2,1)} %shard_map.73) | data formatting | bytes 262144

commit v4 on v3

--- a/solution.py
+++ b/solution.py
@@ -39,6 +39,11 @@
     x_to, z_to = (x_next, x_back), (z_next, z_back)
     z_jump = x * nz + (z + 2) % nz, x * nz + (z + nz - 2) % nz
 
+    barrier = pltpu.get_barrier_semaphore()
+    senders = [(section, t) for t in x_to + z_to + z_jump] + [(s_back, me)]
+    for target in senders:
+        pl.semaphore_signal(barrier, inc=1, device_id=target, device_id_type=MESH)
+
     locals_ = [
         pltpu.make_async_copy(hidden.at[0:rb], xb.at[0, 0, 0], lsem.at[0]),
         pltpu.make_async_copy(hidden.at[rb:rows], xc.at[0, 0, 0], lsem.at[1]),
@@ -58,10 +63,6 @@
         for c in entry:
             c.start()
 
-    barrier = pltpu.get_barrier_semaphore()
-    senders = [(section, t) for t in x_to + z_to + z_jump] + [(s_back, me)]
-    for target in senders:
-        pl.semaphore_signal(barrier, inc=1, device_id=target, device_id_type=MESH)
     pl.semaphore_wait(barrier, len(senders))
 
     sent = []
@@ -239,16 +240,16 @@
             steps = [k + str(s) for s in range(stages) for k in ("CE", "CX", "BE", "BP", "BX", "CA", "CF", "BA", "CK", "BK")]
             steps += [k + str(stages) for k in ("CE", "CX", "BE", "BX", "CA", "CK", "BA", "BK")]
             steps += ["CG" + str(s) for s in range(stages)]
-        acc[...] = jnp.zeros_like(acc)
         loaded = False
         for at, step in enumerate(steps):
-            if tick == 0 and at == 5:
-                positions(0)
+            if at == 5:
+                acc[...] = jnp.zeros_like(acc)
+                if tick == 0:
+                    positions(0)
             if not loaded and step[1] in "FKG":
                 if tick == 0:
                     for c in locals_[2:]:
                         c.wait()
-                    positions(1)
                 else:
                     entered()
                 loaded = True
@@ -267,21 +268,29 @@
             for j in range(nz):
                 lsend[first + j] = part[:, j * 128:(j + 1) * 128]
 
-            def spread(i, carry):
-                dz = (half + (1 - 2 * (i % 2)) * ((i + 1) // 2)) % nz
+            def spread(dz):
                 to = first + (z + dz) % nz
                 pltpu.make_async_remote_copy(
                     src_ref=lsend.at[to], dst_ref=lrecv.at[tick, me], send_sem=lora_ssem.at[tick], recv_sem=lora_rsem.at[tick],
                     device_id=(section, to), device_id_type=MESH).start()
+
+            def pair(i, carry):
+                spread(half - i)
+                spread(half + i)
                 return carry
 
-            lax.fori_loop(0, nz if dx else nz - 1, spread, 0)
+            spread(half)
+            lax.fori_loop(1, half, pair, 0)
+            if dx:
+                spread(0)
         own = pltpu.make_async_copy(lsend.at[me], lrecv.at[tick, me], lsem.at[7])
         own.start()
         own.wait()
         others = pltpu.make_async_remote_copy(
             src_ref=lsend.at[0:nt - 1], dst_ref=lrecv.at[tick, 0:nt - 1], send_sem=lora_ssem.at[tick], recv_sem=lora_rsem.at[tick],
             device_id=(section, x_next), device_id_type=MESH)
+        if tick + 1 < TICKS:
+            positions(tick + 1)
         others.wait_recv()
         lora = jnp.dot(place[tick], lrecv[tick].reshape(nt * CAP, 128), preferred_element_type=F32)
         held = jnp.concatenate([xb[tick, 0, 0], xc[tick, 0, 0]], axis=0).astype(F32)
@@ -335,7 +344,7 @@
     vmem, hbm = pl.BlockSpec(memory_space=pltpu.VMEM), pl.BlockSpec(memory_space=pl.ANY)
     return pl.pallas_call(
         functools.partial(kernel, nz),
-        out_shape=jax.ShapeDtypeStruct((TICKS, rows, cols), BF16),
+        out_shape=pltpu.VMEM((TICKS, rows, cols), BF16),
         in_specs=[hbm, hbm, vmem, vmem, hbm, hbm, hbm],
         out_specs=vmem,
         scratch_shapes=[

time: 108 us -> 107 us (level)
  no operation moved by 1% of the time
where the time goes in v4:
time: 107 us; the launch traced here: 106 us
  Pallas kernels  106 us (99%)
    pallas_call x1, Pallas kernels, local(): pl.pallas_call(functools.partial(kernel, nz), out_shape=pltpu.VMEM((TICKS...  106 us

profile of v4, /device:TPU:32, one launch (start us, length us, event | category | flops | bytes accessed | tf_op | source)
XLA Modules:
  0.0 106.4 jit_solution(10700232863138822091)
XLA Ops:
  0.0 105.7 %shard_map.73 = bf16[2,256,128]{2,1,0:T(8,128)(2,1)S(1)} custom-call(bf16[256,128]{1,0:T(8,128)(2,1)} %hidden.1, bf16[256,128]{1,0:T(8,128)(2,1)} %arriving.1, s32[9,1,256]{2,1,0:T(1,128)} %bitcast.10, s32[1,64]{1,0:T(1,128)} %bitcast.11, bf16[8192,128]{1,0:T(8,128)(2,1)} %bitcast.7, bf16[64,8192]{1,0:T(8,128)(2,1)} %bitcast.8, bf16[64,8192]{1,0:T(8,128)(2,1)} %bitcast.9), custom_call_target="tpu_custom_call" | custom-call | tf_op jit(solution)/shard_map/pallas_call | solution.py:345
  105.8 0.7 copy.9
